TPU v7x, 32 devices: a whole 2x2x4 slice. The times are simulated.
32 devices in a mesh: grp: 2 (over core), fsdp: 8 (over z, y), tp: 2 (over x).
Axes of the slice: x: 2, y: 2, z: 4, core: 2. Of those that a mesh axis runs over, the one named last changes fastest.
Arguments:
- frames: bfloat16 [2, 2048, 8192], P('grp', 'fsdp'), may hold values from -6 to 6
- rewards: bfloat16 [2048], P('fsdp'), may hold values from -5 to 5
- actions: int32 [2, 2048], P('grp', 'fsdp'), may hold values from 0 to 17
- fractions: int32 [2, 2048, 32], P('grp', 'fsdp'), may hold values from 0 to 63
- episode_shard: int32 [2048, 1], P('fsdp'), may hold values from 0 to 7, as said below
- table: float32 [64], replicated, may hold values from 0.02 to 0.98
- norm_gain: float32 [8192], replicated, may hold values from 0.1 to 1.9
- torso_weight: bfloat16 [8192, 4096], P(('grp', 'fsdp'), 'tp'), may hold values from -0.0625 to 0.0625
- embed_weight: bfloat16 [64, 4096], P(None, 'tp'), may hold values from -0.75 to 0.75
- value_weight: bfloat16 [18, 4096], P(None, 'tp'), may hold values from -0.59765625 to 0.59765625
Outputs:
- torso_grad: float32 [8192, 4096], P(('grp', 'fsdp'), 'tp')
- refreshed_weight: bfloat16 [8192, 4096], P(('grp', 'fsdp', 'tp'))
Inputs may be any that keep to these rules, and one draw needn't show every extreme that they name: `episode_shard`: of the rows of one index of fsdp, at most 48 belong to one learner shard, and in every such block some learner shard gets exactly 48; every learner shard gets at least one row from every block.
All inputs are finite; a program needn't handle non-finite values.
Results may differ from a plain program's by a relative error of at most 0.0075.
Values may be sent and summed in bfloat16 or wider, within the bound.
A program may use at most 128 MiB of HBM per device.

v0:
```python
import jax
import jax.numpy as jnp
from jax import lax
from jax.sharding import PartitionSpec as P

ACTIONS = 18
COSINES = 64
FRACS = 64


def from_partner(value, axis, bit):
    mask = 2**bit
    pairs = [(source, source ^ mask) for source in range(lax.axis_size(axis))]
    return lax.ppermute(value, axis, pairs)


def shards(
    frames,
    rewards,
    actions,
    fractions,
    episode_shard,
    table,
    norm_gain,
    torso_weight,
    embed_weight,
    value_weight,
):
    shard_total = lax.axis_size("fsdp")
    destination = episode_shard[:, 0]
    rows_block = destination.shape[0]
    lanes = jnp.arange(shard_total, dtype=jnp.int32)
    onehot = (destination[:, None] == lanes[None, :]).astype(jnp.int32)
    counts = lax.psum(jnp.sum(onehot.astype(jnp.float32), axis=0), "fsdp")
    row_weight = jnp.dot(
        onehot.astype(jnp.float32), float(rows_block) / counts, precision=lax.Precision.HIGHEST
    )
    rows_data = frames[0]
    action_rows = actions[0]
    fraction_rows = fractions[0]
    values = rows_data.astype(jnp.float32)
    mean_square = jnp.mean(values * values, axis=-1, keepdims=True)
    normed = (values * lax.rsqrt(mean_square + 1e-05) * norm_gain).astype(jnp.bfloat16)
    preact = jnp.dot(
        normed,
        lax.all_gather(torso_weight, ("grp", "fsdp"), axis=0, tiled=True),
        preferred_element_type=jnp.float32,
    )
    choose_mask = (action_rows[:, None] == jnp.arange(ACTIONS, dtype=jnp.int32)[None, :]).astype(
        jnp.bfloat16
    )
    picked = jnp.dot(choose_mask, value_weight, preferred_element_type=jnp.float32)
    weighted = (jax.nn.silu(preact) * picked).astype(jnp.bfloat16)
    cosine = jnp.cos(
        jnp.pi * jnp.arange(COSINES, dtype=jnp.float32)[None, :] * table[:, None]
    ).astype(jnp.bfloat16)
    embedding = jax.nn.relu(
        jnp.dot(cosine, embed_weight, preferred_element_type=jnp.float32)
    ).astype(jnp.bfloat16)
    table_values = lax.dot_general(
        weighted, embedding, (((1,), (1,)), ((), ())), preferred_element_type=jnp.float32
    )
    selector = (
        fraction_rows[:, :, None] == jnp.arange(FRACS, dtype=jnp.int32)[None, None, :]
    ).astype(jnp.float32)
    partial_quant = jnp.einsum(
        "mj,mtj->mt", table_values, selector, precision=lax.Precision.HIGHEST
    )
    group_index = lax.axis_index("grp")
    own_slot = jnp.arange(2, dtype=jnp.int32)[:, None, None] == group_index
    stacked = jnp.where(
        own_slot, partial_quant[None, :, :], jnp.zeros_like(partial_quant)[None, :, :]
    )
    summed = lax.psum(stacked, ("grp", "tp"))
    target_quant = summed[0]
    online_quant = summed[1]
    learner = (group_index == 1).astype(jnp.float32)
    levels = jnp.einsum("mtj,j->mt", selector, table, precision=lax.Precision.HIGHEST)
    target_value = rewards.astype(jnp.float32)[:, None] + 0.99 * target_quant
    errors = target_value[:, None, :] - online_quant[:, :, None]
    weight = jnp.abs(levels[:, :, None] - (errors < 0).astype(jnp.float32))
    grad_quant = -(learner * row_weight)[:, None] * jnp.sum(
        weight * jnp.clip(errors, -1.0, 1.0), axis=-1
    )
    grad_table = jnp.einsum("mi,mij->mj", grad_quant, selector, precision=lax.Precision.HIGHEST)
    grad_feature = jnp.dot(
        grad_table, embedding.astype(jnp.float32), precision=lax.Precision.HIGHEST
    )
    gate_value = jax.nn.sigmoid(preact)
    grad_preact = (grad_feature * picked * gate_value * (1.0 + preact * (1.0 - gate_value))).astype(
        jnp.bfloat16
    )
    block = torso_weight.shape[0]
    rows_here = normed.shape[0]
    arranged = normed.reshape(rows_here, 2, shard_total, block).transpose(2, 1, 0, 3)
    arranged = arranged.transpose(0, 2, 1, 3).reshape(shard_total, rows_here, 2 * block)
    columns_all = lax.all_to_all(arranged, "fsdp", split_axis=0, concat_axis=0, tiled=True).reshape(
        shard_total * rows_here, 2 * block
    )
    both_blocks = lax.dot_general(
        columns_all,
        lax.all_gather(grad_preact, "fsdp", axis=0, tiled=True),
        (((0,), (0,)), ((), ())),
        preferred_element_type=jnp.float32,
    )
    partner = from_partner(both_blocks[:block], "grp", 0)
    torso_grad = jnp.where(group_index == 1, both_blocks[block:], partner)
    updated = (torso_weight.astype(jnp.float32) - 0.01 * torso_grad).astype(jnp.bfloat16)
    refreshed_weight = lax.all_to_all(updated, "tp", split_axis=0, concat_axis=1, tiled=True)
    return (torso_grad, refreshed_weight)


def solution(mesh):
    placed = (
        P("grp", "fsdp", None),
        P("fsdp"),
        P("grp", "fsdp"),
        P("grp", "fsdp", None),
        P("fsdp", None),
        P(),
        P(),
        P(("grp", "fsdp"), "tp"),
        P(None, "tp"),
        P(None, "tp"),
    )
    return jax.shard_map(
        shards,
        mesh=mesh,
        in_specs=placed,
        out_specs=(P(("grp", "fsdp"), "tp"), P(("grp", "fsdp", "tp"), None)),
        check_vma=False,
    )
```

profile of v0, /device:TPU:0, one launch (start us, length us, event | category | flops | bytes accessed | tf_op | source)
XLA Modules:
  0.0 500.6 jit_solution(17945190309023998001)
XLA Ops:
  8.0 0.8 convert_reduce_fusion
  8.8 23.3 %psum.14 = f32[8]{0:T(128)S(1)} all-reduce(f32[8]{0:T(128)S(1)} %convert_reduce_fusion), channel_id=1, replica_groups=mesh['grp'=2,'fsdp'=8,'tp'=2] {'fsdp'}, use_global_device_ids=true, to_apply=%region_2.0 | all-reduce | flops 8 | bytes 64 | tf_op jit(solution)/shard_map/psum | solution.py:34
  32.1 6.4 %copy.26 = bf16[1,256,8192]{1,2,0:T(8,128)(2,1)} copy(bf16[1,256,8192]{2,1,0:T(8,128)(2,1)} %param.10) | data formatting | bytes 8388608 | tf_op args[0]
  38.5 3.6 fusion
  42.7 1.8 fusion.21
  44.5 3.7 fusion.17
  48.3 132.2 %all-gather.3.cloned.1.call-done = bf16[8192,2048]{1,0:T(8,128)(2,1)} async-done(((bf16[512,2048]{1,0:T(8,128)(2,1)}), bf16[8192,2048]{1,0:T(8,128)(2,1)}) %all-gather.3.cloned.1.call-update) | async-done | bytes 33554448 | tf_op jit(solution)/shard_map/all_gather | solution.py:46
  180.5 16.4 %fusion.4 = f32[256,2048]{1,0:T(8,128)S(1)} fusion(bf16[8192,2048]{1,0:T(8,128)(2,1)} %all-gather.3.cloned.1.call-done, bf16[1,256,8192]{1,2,0:T(8,128)(2,1)} %copy.26, f32[8192]{0:T(1024)S(1)} %copy-done.4, f32[256]{0:T(256)S(1)} %add_rsqrt_fusion), kind=kOutput, calls=%fused_computation.7 | convolution fusion | flops 8598323200 | bytes 39879680 | tf_op jit(solution)/shard_map/dot_general | solution.py:44
  196.9 2.3 fusion.20
  199.6 0.7 broadcast_select_fusion
  200.5 2.8 copy.30
  203.4 28.2 %all-reduce.2.cloned.1.call-done = f32[2,256,32]{1,2,0:T(8,128)} async-done(((f32[2,256,32]{1,2,0:T(8,128)}), f32[2,256,32]{1,2,0:T(8,128)}) %all-reduce.2.cloned.1.call-update) | async-done | bytes 65552 | tf_op jit(solution)/shard_map/psum | solution.py:74
  231.6 0.8 slice_bitcast_fusion
  232.4 0.8 fusion.24
  233.9 4.2 fusion.11
  238.2 2.9 fusion.3
  241.4 190.2 %all_to_all.24 = bf16[8,256,1024]{1,2,0:T(8,128)(2,1)} all-to-all(bf16[8,256,1024]{1,2,0:T(8,128)(2,1)S(1)} %bitcast.50), channel_id=1, replica_groups=mesh['grp'=2,'fsdp'=8,'tp'=2] {'fsdp'}, dimensions={0} | all-to-all | bytes 8388608 | tf_op jit(solution)/shard_map/all_to_all | solution.py:97
  431.6 6.4 %copy.28 = bf16[8,256,1024]{2,1,0:T(8,128)(2,1)} copy(bf16[8,256,1024]{1,2,0:T(8,128)(2,1)} %all_to_all.24) | data formatting | bytes 8388608 | tf_op jit(solution)/shard_map/all_to_all | solution.py:97
  438.0 2.4 all-gather.5.cloned.1.call-done
  440.5 13.0 %fusion.37 = f32[1024,2048]{1,0:T(8,128)S(1)} fusion(bf16[2048,1024]{1,0:T(8,128)(2,1)} %bitcast.53, bf16[2048,2048]{1,0:T(8,128)(2,1)} %all-gather.5.cloned.1.call-done), kind=kOutput, calls=%fused_computation.61 | convolution fusion | flops 8589934592 | bytes 20971520 | tf_op jit(solution)/shard_map/dot_general | solution.py:100
  454.1 7.1 %collective-permute-done = f32[512,2048]{1,0:T(8,128)S(1)} collective-permute-done((f32[512,2048]{1,0:T(8,128)S(1)}, f32[512,2048]{1,0:T(8,128)S(1)}, u32[]{:S(2)}, u32[]{:S(2)}) %collective-permute-start) | collective-permute-done | bytes 4194336 | tf_op jit(solution)/shard_map/ppermute | solution.py:14
  461.2 3.3 subtract_convert_fusion
  464.5 28.1 %all_to_all.25 = bf16[2,256,2048]{2,1,0:T(8,128)(2,1)S(1)} all-to-all(bf16[2,256,2048]{2,1,0:T(8,128)(2,1)S(1)} %bitcast.51), channel_id=1, replica_groups=mesh['grp'=2,'fsdp'=8,'tp'=2] {'tp'}, dimensions={0} | all-to-all | bytes 4194304 | tf_op jit(solution)/shard_map/all_to_all | solution.py:109
  492.6 1.5 copy.44
  (41 shorter events, 3.7 us)
Async XLA Ops:
  7.2 35.2 %copy-start = (bf16[64,2048]{1,0:T(8,128)(2,1)S(1)}, bf16[64,2048]{1,0:T(8,128)(2,1)}, u32[]{:S(2)}) copy-start(bf16[64,2048]{1,0:T(8,128)(2,1)} %param.18) | copy-start | bytes 786436
  7.2 173.3 %all-gather.3.cloned.1.call-start = ((), (), s32[]{:S(2)}) async-start(), calls=%async_computation.2 | async-start | bytes 35651584 | tf_op jit(solution)/shard_map/all_gather | solution.py:46
  7.9 223.7 %all-reduce.2.cloned.1.call-start = ((), (), s32[]{:S(2)}) async-start(), calls=%async_computation.3 | async-start | bytes 131072 | tf_op jit(solution)/shard_map/psum | solution.py:74
  38.5 3.7 copy-start.8
  38.5 3.9 copy-start.6
  38.5 4.3 copy-start.5
  38.5 4.3 copy-start.7
  38.5 6.1 %copy-start.3 = (s32[1,256,32]{1,2,0:T(8,128)S(1)}, s32[1,256,32]{1,2,0:T(8,128)}, u32[]{:S(2)}) copy-start(s32[1,256,32]{1,2,0:T(8,128)} %param.13) | copy-start | bytes 98308
  42.2 138.3 %copy-start.4 = (f32[8192]{0:T(1024)S(1)}, f32[8192]{0:T(1024)}, u32[]{:S(2)}) copy-start(f32[8192]{0:T(1024)} %param.16) | copy-start | bytes 98308
  196.9 3.6 copy-start.9
  200.3 240.2 %all-gather.5.cloned.1.call-start = ((), (), s32[]{:S(2)}) async-start(), calls=%async_computation.4 | async-start | bytes 9437184 | tf_op jit(solution)/shard_map/all_gather | solution.py:102
  453.5 7.7 %copy-start.2 = (bf16[512,2048]{1,0:T(8,128)(2,1)S(1)}, bf16[512,2048]{1,0:T(8,128)(2,1)}, u32[]{:S(2)}) copy-start(bf16[512,2048]{1,0:T(8,128)(2,1)} %param.17) | copy-start | bytes 6291460
  454.0 7.2 %collective-permute-start = (f32[512,2048]{1,0:T(8,128)S(1)}, f32[512,2048]{1,0:T(8,128)S(1)}, u32[]{:S(2)}, u32[]{:S(2)}) collective-permute-start(f32[512,2048]{1,0:T(8,128)S(1)} %slice.19), channel_id=1, source_target_pairs={{0,16},{16,0},{1,17},{17,1},{2,18},{18,2},{3,19},{19,3},{4,20},{20... | collective-permute-start | bytes 12582920 | tf_op jit(solution)/shard_map/ppermute | solution.py:14
  464.5 29.5 %copy-start.1 = (bf16[64,2048]{1,0:T(8,128)(2,1)S(1)}, bf16[64,2048]{1,0:T(8,128)(2,1)}, u32[]{:S(2)}) copy-start(bf16[64,2048]{1,0:T(8,128)(2,1)} %param.18) | copy-start | bytes 786436
Sparse Core Ops, SparseCore 0:
  9.6 170.8 all-gather.2
  200.4 31.1 all-reduce.1
  238.3 202.1 all-gather.4
where the time goes:
time: 501 us
  blocking collectives  242 us (48%)
  waiting for transfers between devices  171 us (34%)
  matrix products  42 us (8%)
  local copies, waits for them, and re-layouts  18.8 us (4%)
  between operations  13.9 us (3%)
  other arithmetic  13.2 us (3%)
    all_to_all x1, blocking collectives, shards(): lax.all_to_all(arranged, 'fsdp', split_axis=0, concat_axis=0, tiled=True)  190 us
    all_gather x1, waiting for transfers between devices, shards(): lax.all_gather(torso_weight, ('grp', 'fsdp'), axis=0, tiled=True)  132 us
    psum x1, waiting for transfers between devices, shards(): summed = lax.psum(stacked, ('grp', 'tp'))  28.2 us
    all_to_all x1, blocking collectives, shards(): lax.all_to_all(updated, 'tp', split_axis=0, concat_axis=1, tiled=True)  28.1 us
    psum x1, blocking collectives, shards(): counts = lax.psum(jnp.sum(onehot.astype(jnp.float32), axis=0), 'fsdp')  23.3 us
    dot_general x1, matrix products, shards(): jnp.dot(normed, lax.all_gather(torso_weight, ('grp', 'fsdp'), axis=0, til...  16.4 us
    dot_general x1, matrix products, shards(): lax.dot_general(columns_all, lax.all_gather(grad_preact, 'fsdp', axis=0,...  13 us
  transfers between devices with their start and end apart: 4, of which 4 were waited for; matrix products, arithmetic and copies ran while one was open for 6% of the time, Pallas kernels for 0%

commit v1 on v0

v1 whole, which is shorter than its diff:
```python
import jax
import jax.numpy as jnp
from jax import lax
from jax.sharding import PartitionSpec as P

ACTIONS = 18
COSINES = 64
FRACS = 64
PARTS = (2, 1, 1)


def rotate(value, axis, step):
    size = lax.axis_size(axis)
    return lax.ppermute(value, axis, [(s, (s + step) % size) for s in range(size)])


def swap_half(value, group_index):
    half = value.shape[0] // 2
    kept = lax.dynamic_slice_in_dim(value, group_index * half, half, 0)
    sent = lax.dynamic_slice_in_dim(value, (1 - group_index) * half, half, 0)
    got = rotate(sent, "grp", 1)
    first = group_index == 0
    return jnp.concatenate([jnp.where(first, kept, got), jnp.where(first, got, kept)], axis=0)


def arrange(pieces, index):
    total = len(pieces)
    blocks = []
    for source in range(total):
        offset = lax.rem(index - source + total, total)
        block = pieces[0]
        for step in range(1, total):
            block = jnp.where(offset == step, pieces[step], block)
        blocks.append(block)
    return blocks


def bounds(columns):
    unit = columns // sum(PARTS)
    result, start = [], 0
    for part in PARTS:
        result.append((start, start + part * unit))
        start += part * unit
    return result


def shards(
    frames,
    rewards,
    actions,
    fractions,
    episode_shard,
    table,
    norm_gain,
    torso_weight,
    embed_weight,
    value_weight,
):
    shard_total = lax.axis_size("fsdp")
    tp_total = lax.axis_size("tp")
    group_index = lax.axis_index("grp")
    tp_index = lax.axis_index("tp")
    block, columns = torso_weight.shape
    spans = bounds(columns)
    gathered = [
        lax.all_gather(torso_weight[:, a:b], ("grp", "fsdp"), axis=0, tiled=True) for a, b in spans
    ]

    rows_block = episode_shard.shape[0]
    half = rows_block // 2
    destination = episode_shard[:, 0]
    lanes = jnp.arange(shard_total, dtype=jnp.int32)
    onehot = (destination[:, None] == lanes[None, :]).astype(jnp.float32)
    counts = lax.psum(jnp.sum(onehot, axis=0), "fsdp")
    row_weight = jnp.dot(
        lax.dynamic_slice_in_dim(onehot, group_index * half, half, 0),
        float(rows_block) / counts,
        precision=lax.Precision.HIGHEST,
    )
    reward_rows = lax.dynamic_slice_in_dim(rewards, group_index * half, half, 0)

    action_rows = swap_half(actions[0], group_index)
    fraction_rows = swap_half(fractions[0], group_index)
    values = swap_half(frames[0], group_index).astype(jnp.float32)
    mean_square = jnp.mean(values * values, axis=-1, keepdims=True)
    normed = (values * lax.rsqrt(mean_square + 1e-05) * norm_gain).astype(jnp.bfloat16)

    rows_part = half // tp_total
    own_rows = lax.dynamic_slice_in_dim(normed, half + tp_index * rows_part, rows_part, 0)
    outgoing = own_rows.reshape(rows_part, 2 * shard_total, block).transpose(1, 0, 2)
    incoming = lax.all_to_all(outgoing, ("grp", "fsdp"), split_axis=0, concat_axis=0, tiled=True)
    pieces = [incoming] + [rotate(incoming, "tp", step) for step in range(1, tp_total)]
    columns_all = jnp.concatenate(
        [piece[:, None] for piece in arrange(pieces, tp_index)], axis=1
    ).reshape(2 * shard_total * half, block)

    choose_mask = (action_rows[:, None] == jnp.arange(ACTIONS, dtype=jnp.int32)[None, :]).astype(
        jnp.bfloat16
    )
    picked = jnp.dot(choose_mask, value_weight, preferred_element_type=jnp.float32)
    cosine = jnp.cos(
        jnp.pi * jnp.arange(COSINES, dtype=jnp.float32)[None, :] * table[:, None]
    ).astype(jnp.bfloat16)
    embedding = jax.nn.relu(
        jnp.dot(cosine, embed_weight, preferred_element_type=jnp.float32)
    ).astype(jnp.bfloat16)
    selector = (
        fraction_rows[:, :, None] == jnp.arange(FRACS, dtype=jnp.int32)[None, None, :]
    ).astype(jnp.float32)
    levels = jnp.einsum("mtj,j->mt", selector[half:], table, precision=lax.Precision.HIGHEST)

    gathered[0], columns_all, picked, embedding, levels, row_weight = lax.optimization_barrier(
        (gathered[0], columns_all, picked, embedding, levels, row_weight)
    )
    table_values = None
    preacts = []
    for (a, b), weight_columns in zip(spans, gathered):
        preact = jnp.dot(normed, weight_columns, preferred_element_type=jnp.float32)
        weighted = (jax.nn.silu(preact) * picked[:, a:b]).astype(jnp.bfloat16)
        term = lax.dot_general(
            weighted,
            embedding[:, a:b],
            (((1,), (1,)), ((), ())),
            preferred_element_type=jnp.float32,
        )
        table_values = term if table_values is None else table_values + term
        preacts.append(preact[half:])

    quant = jnp.einsum("mj,mtj->mt", table_values, selector, precision=lax.Precision.HIGHEST)
    others = [rotate(quant, "tp", step) for step in range(1, tp_total)]
    for other in others:
        quant = quant + other
    target_quant, online_quant = quant[:half], quant[half:]
    target_value = reward_rows.astype(jnp.float32)[:, None] + 0.99 * target_quant
    errors = target_value[:, None, :] - online_quant[:, :, None]
    weight = jnp.abs(levels[:, :, None] - (errors < 0).astype(jnp.float32))
    grad_quant = -row_weight[:, None] * jnp.sum(weight * jnp.clip(errors, -1.0, 1.0), axis=-1)
    grad_table = jnp.einsum(
        "mi,mij->mj", grad_quant, selector[half:], precision=lax.Precision.HIGHEST
    )

    rows_all = []
    for (a, b), preact in zip(spans, preacts):
        grad_feature = jnp.dot(
            grad_table, embedding[:, a:b].astype(jnp.float32), precision=lax.Precision.HIGHEST
        )
        gate_value = jax.nn.sigmoid(preact)
        grad_preact = (
            grad_feature * picked[half:, a:b] * gate_value * (1.0 + preact * (1.0 - gate_value))
        ).astype(jnp.bfloat16)
        rows_all.append(lax.all_gather(grad_preact, ("grp", "fsdp"), axis=0, tiled=True))

    grads = []
    refreshed = [[] for _ in range(tp_total)]
    share = block // tp_total
    for (a, b), rows in zip(spans, rows_all):
        grad = lax.dot_general(
            columns_all, rows, (((0,), (0,)), ((), ())), preferred_element_type=jnp.float32
        )
        updated = (torso_weight[:, a:b].astype(jnp.float32) - 0.01 * grad).astype(jnp.bfloat16)
        pieces = []
        for step in range(tp_total):
            target = lax.rem(tp_index + step, tp_total)
            piece = lax.dynamic_slice_in_dim(updated, target * share, share, 0)
            pieces.append(rotate(piece, "tp", step) if step else piece)
        for source, piece in enumerate(arrange(pieces, tp_index)):
            refreshed[source].append(piece)
        grads.append(grad)
    torso_grad = jnp.concatenate(grads, axis=1)
    refreshed_weight = jnp.concatenate([piece for row in refreshed for piece in row], axis=1)
    return (torso_grad, refreshed_weight)


def solution(mesh):
    placed = (
        P("grp", "fsdp", None),
        P("fsdp"),
        P("grp", "fsdp"),
        P("grp", "fsdp", None),
        P("fsdp", None),
        P(),
        P(),
        P(("grp", "fsdp"), "tp"),
        P(None, "tp"),
        P(None, "tp"),
    )
    return jax.shard_map(
        shards,
        mesh=mesh,
        in_specs=placed,
        out_specs=(P(("grp", "fsdp"), "tp"), P(("grp", "fsdp", "tp"), None)),
        check_vma=False,
    )
```

time: 501 us -> 494 us (0.986)
  blocking collectives: 242 us -> 38.7 us
  waiting for transfers between devices: 171 us -> 356 us
  starting transfers between devices: 0.43 us -> 15.5 us
  local copies, waits for them, and re-layouts: 18.8 us -> 12.7 us
    all_to_all x2 -> x0, blocking collectives: 218 us -> none  [the longest x1 190 us: shards(): lax.all_to_all(arranged, 'fsdp', split_axis=0, concat_axis=0, tiled=True)]
    all_gather x2 -> x6, waiting for transfers between devices: 135 us -> 307 us  [the longest x3 186 us: shards(): lax.all_gather(torso_weight[:, a:b], ('grp', 'fsdp'), axis=0, tiled=True)]
    ppermute x1 -> x8, waiting for transfers between devices: 7.09 us -> 46.1 us  [rotate(): lax.ppermute(value, axis, [(s, (s + step) % size) for s in range(size)])]
    psum x1 -> x0, waiting for transfers between devices: 28.2 us -> none  [shards(): summed = lax.psum(stacked, ('grp', 'tp'))]
    psum x1, blocking collectives: 23.3 us -> 38.7 us  [shards(): counts = lax.psum(jnp.sum(onehot, axis=0), 'fsdp')]
    all_to_all x2 -> x0, local copies, waits for them, and re-layouts: 7.88 us -> none  [the longest x1 6.43 us: shards(): lax.all_to_all(arranged, 'fsdp', split_axis=0, concat_axis=0, tiled=True)]
    ppermute x1 -> x8, starting transfers between devices: 0.13 us -> 7.79 us  [rotate(): lax.ppermute(value, axis, [(s, (s + step) % size) for s in range(size)])]
    all_to_all x0 -> x1, starting transfers between devices: none -> 7.28 us  [shards(): lax.all_to_all(outgoing, ('grp', 'fsdp'), split_axis=0, concat_axis=0, ti...]
  transfers between devices with their start and end apart: 4 -> 15, of which waited for: 4 -> 12; matrix products, arithmetic and copies ran while one was open for 6% -> 9% of each run, Pallas kernels for 0% -> 0%
where the time goes in v1:
time: 494 us
  waiting for transfers between devices  356 us (72%)
  matrix products  46.4 us (9%)
  blocking collectives  38.7 us (8%)
  starting transfers between devices  15.5 us (3%)
  between operations  14.5 us (3%)
  local copies, waits for them, and re-layouts  12.7 us (3%)
  other arithmetic  9.58 us (2%)
    all_gather x3, waiting for transfers between devices, shards(): lax.all_gather(torso_weight[:, a:b], ('grp', 'fsdp'), axis=0, tiled=True)  186 us
    all_gather x3, waiting for transfers between devices, shards(): lax.all_gather(grad_preact, ('grp', 'fsdp'), axis=0, tiled=True)  121 us
    ppermute x8, waiting for transfers between devices, rotate(): lax.ppermute(value, axis, [(s, (s + step) % size) for s in range(size)])  46.1 us
    psum x1, blocking collectives, shards(): counts = lax.psum(jnp.sum(onehot, axis=0), 'fsdp')  38.7 us
    dot_general x3, matrix products, shards(): preact = jnp.dot(normed, weight_columns, preferred_element_type=jnp.float32)  25.1 us
    dot_general x3, matrix products, shards(): lax.dot_general(columns_all, rows, (((0,), (0,)), ((), ())), preferred_el...  12.2 us
  transfers between devices with their start and end apart: 15, of which 12 were waited for; matrix products, arithmetic and copies ran while one was open for 9% of the time, Pallas kernels for 0%

profile of v1, /device:TPU:0, one launch (start us, length us, event | category | flops | bytes accessed | tf_op | source)
XLA Modules:
  0.0 493.7 jit_solution(11182760013348467544)
XLA Ops:
  7.2 2.4 fusion.40
  11.6 3.1 dynamic-slice_bitcast_fusion
  15.1 4.0 collective-permute-done
  19.1 2.6 bitcast_select_fusion.1
  27.7 7.3 %all-to-all-start = ((bf16[16,64,512]{2,1,0:T(8,128)(2,1)}), bf16[16,64,512]{2,1,0:T(8,128)(2,1)S(1)}, u32[]{:S(2)}, u32[]{:S(2)}) async-start(bf16[16,64,512]{2,1,0:T(8,128)(2,1)} %copy.39), calls=%async_computation | async-start | bytes 2097152 | tf_op jit(solution)/shard_map/all_to_all | solution.py:91
  35.8 38.7 %psum.7 = f32[8]{0:T(128)S(1)} all-reduce(f32[8]{0:T(128)S(1)} %convert_reduce_fusion), channel_id=1, replica_groups=mesh['grp'=2,'fsdp'=8,'tp'=2] {'fsdp'}, use_global_device_ids=true, to_apply=%region_2.3 | all-reduce | flops 8 | bytes 64 | tf_op jit(solution)/shard_map/psum | solution.py:74
  75.1 2.5 all-to-all-done
  81.5 20.8 %collective-permute-done.1 = bf16[16,64,512]{2,1,0:T(8,128)(2,1)S(1)} collective-permute-done((bf16[16,64,512]{2,1,0:T(8,128)(2,1)S(1)}, bf16[16,64,512]{2,1,0:T(8,128)(2,1)S(1)}, u32[]{:S(2)}, u32[]{:S(2)}) %collective-permute-start.1) | collective-permute-done | bytes 1048608 | tf_op jit(solution)/shard_map/ppermute | solution.py:14
  102.6 7.8 %fusion.42 = f32[256,512]{1,0:T(8,128)} fusion(bf16[256,8192]{1,0:T(8,128)(2,1)} %copy-done.2, bf16[8192,512]{1,0:T(8,128)(2,1)} %all-gather.9.cloned.1.call-done), kind=kOutput, calls=%fused_computation.99 | convolution fusion | flops 2147483648 | bytes 13107200 | tf_op jit(solution)/shard_map/dot_general | solution.py:118
  110.4 66.1 %all-gather.11.cloned.1.call-done = bf16[8192,512]{1,0:T(8,128)(2,1)} async-done(((bf16[512,512]{1,0:T(8,128)(2,1)}), bf16[8192,512]{1,0:T(8,128)(2,1)}) %all-gather.11.cloned.1.call-update) | async-done | bytes 8388624 | tf_op jit(solution)/shard_map/all_gather | solution.py:66
  176.5 7.8 %fusion.43 = f32[256,512]{1,0:T(8,128)} fusion(bf16[256,8192]{1,0:T(8,128)(2,1)} %copy-done.2, bf16[8192,512]{1,0:T(8,128)(2,1)} %all-gather.11.cloned.1.call-done), kind=kOutput, calls=%fused_computation.100 | convolution fusion | flops 2147483648 | bytes 13107200 | tf_op jit(solution)/shard_map/dot_general | solution.py:118
  184.3 119.6 %all-gather.7.cloned.1.call-done = bf16[8192,1024]{1,0:T(8,128)(2,1)} async-done(((bf16[512,1024]{1,0:T(8,128)(2,1)}), bf16[8192,1024]{1,0:T(8,128)(2,1)}) %all-gather.7.cloned.1.call-update) | async-done | bytes 16777232 | tf_op jit(solution)/shard_map/all_gather | solution.py:66
  303.9 9.5 %fusion.41 = f32[256,1024]{1,0:T(8,128)S(1)} fusion(bf16[256,8192]{1,0:T(8,128)(2,1)} %copy-done.2, bf16[8192,1024]{1,0:T(8,128)(2,1)} %all-gather.7.cloned.1.call-done), kind=kOutput, calls=%fused_computation.98 | convolution fusion | flops 4294967296 | bytes 22020096 | tf_op jit(solution)/shard_map/dot_general | solution.py:118
  317.6 2.4 collective-permute-done.4
  323.7 2.5 fusion.6
  326.2 34.9 %all-gather.15.cloned.1.call-done = bf16[2048,512]{1,0:T(8,128)(2,1)} async-done(((bf16[128,512]{1,0:T(8,128)(2,1)}), bf16[2048,512]{1,0:T(8,128)(2,1)}) %all-gather.15.cloned.1.call-update) | async-done | bytes 2097168 | tf_op jit(solution)/shard_map/all_gather | solution.py:151
  361.1 2.9 fusion.44
  363.9 39.4 %all-gather.17.cloned.1.call-done = bf16[2048,512]{1,0:T(8,128)(2,1)} async-done(((bf16[128,512]{1,0:T(8,128)(2,1)}), bf16[2048,512]{1,0:T(8,128)(2,1)}) %all-gather.17.cloned.1.call-update) | async-done | bytes 2097168 | tf_op jit(solution)/shard_map/all_gather | solution.py:151
  403.3 4.4 subtract_convert_fusion.1
  407.8 47.0 %all-gather.13.cloned.1.call-done = bf16[2048,1024]{1,0:T(8,128)(2,1)} async-done(((bf16[128,1024]{1,0:T(8,128)(2,1)}), bf16[2048,1024]{1,0:T(8,128)(2,1)}) %all-gather.13.cloned.1.call-update) | async-done | bytes 4194320 | tf_op jit(solution)/shard_map/all_gather | solution.py:151
  454.7 4.9 subtract_convert_fusion
  465.8 8.7 %collective-permute-done.5 = bf16[256,1024]{1,0:T(8,128)(2,1)S(1)} collective-permute-done((bf16[256,1024]{1,0:T(8,128)(2,1)S(1)}, bf16[256,1024]{1,0:T(8,128)(2,1)S(1)}, u32[]{:S(2)}, u32[]{:S(2)}) %collective-permute-start.5) | collective-permute-done | bytes 524320 | tf_op jit(solution)/shard_map/ppermute | solution.py:14
  474.8 5.4 %collective-permute-done.6 = bf16[256,512]{1,0:T(8,128)(2,1)S(1)} collective-permute-done((bf16[256,512]{1,0:T(8,128)(2,1)S(1)}, bf16[256,512]{1,0:T(8,128)(2,1)S(1)}, u32[]{:S(2)}, u32[]{:S(2)}) %collective-permute-start.6) | collective-permute-done | bytes 262176 | tf_op jit(solution)/shard_map/ppermute | solution.py:14
  480.2 4.9 collective-permute-done.7
  (107 shorter events, 29.9 us)
Async XLA Ops:
  7.2 67.5 %copy-start = (bf16[64,2048]{1,0:T(8,128)(2,1)S(1)}, bf16[64,2048]{1,0:T(8,128)(2,1)}, u32[]{:S(2)}) copy-start(bf16[64,2048]{1,0:T(8,128)(2,1)} %param.18) | copy-start | bytes 786436
  7.2 95.4 %all-gather.9.cloned.1.call-start = ((), (), s32[]{:S(2)}) async-start(), calls=%async_computation.2 | async-start | bytes 8912896 | tf_op jit(solution)/shard_map/all_gather | solution.py:66
  9.7 166.9 %all-gather.11.cloned.1.call-start = ((), (), s32[]{:S(2)}) async-start(), calls=%async_computation.3 | async-start | bytes 8912896 | tf_op jit(solution)/shard_map/all_gather | solution.py:66
  10.4 293.5 %all-gather.7.cloned.1.call-start = ((), (), s32[]{:S(2)}) async-start(), calls=%async_computation.1 | async-start | bytes 17825792 | tf_op jit(solution)/shard_map/all_gather | solution.py:66
  14.7 4.5 collective-permute-start
  26.1 8.9 %copy-start.11 = (s32[1,256,32]{1,2,0:T(8,128)S(1)}, s32[1,256,32]{1,2,0:T(8,128)}, u32[]{:S(2)}) copy-start(s32[1,256,32]{1,2,0:T(8,128)} %param.13) | copy-start | bytes 98308
  26.1 9.4 %copy-start.14 = (s32[1,256]{1,0:T(1,128)S(1)}, s32[1,256]{1,0:T(1,128)}, u32[]{:S(2)}) copy-start(s32[1,256]{1,0:T(1,128)} %param.12) | copy-start | bytes 3076
  26.1 9.4 %copy-start.12 = (s32[256,1]{0,1:T(1,128)S(1)}, s32[256,1]{0,1:T(1,128)}, u32[]{:S(2)}) copy-start(s32[256,1]{0,1:T(1,128)} %param.14) | copy-start | bytes 3076
  26.1 48.5 %copy-start.13 = (f32[64]{0:T(128)S(1)}, f32[64]{0:T(128)}, u32[]{:S(2)}) copy-start(f32[64]{0:T(128)} %param.15) | copy-start | bytes 772
  26.1 52.9 %copy-start.9 = (bf16[18,2048]{1,0:T(8,128)(2,1)S(1)}, bf16[18,2048]{1,0:T(8,128)(2,1)}, u32[]{:S(2)}) copy-start(bf16[18,2048]{1,0:T(8,128)(2,1)} %param.19) | copy-start | bytes 221188
  27.7 49.8 %all-to-all-start = ((bf16[16,64,512]{2,1,0:T(8,128)(2,1)}), bf16[16,64,512]{2,1,0:T(8,128)(2,1)S(1)}, u32[]{:S(2)}, u32[]{:S(2)}) async-start(bf16[16,64,512]{2,1,0:T(8,128)(2,1)} %copy.39), calls=%async_computation | async-start | bytes 2097152 | tf_op jit(solution)/shard_map/all_to_all | solution.py:91
  35.0 326.1 %all-gather.15.cloned.1.call-start = ((), (), s32[]{:S(2)}) async-start(), calls=%async_computation.5 | async-start | bytes 2228224 | tf_op jit(solution)/shard_map/all_gather | solution.py:151
  35.1 45.8 %collective-permute-start.3 = (s32[128,32]{0,1:T(8,128)S(1)}, s32[128,32]{0,1:T(8,128)S(1)}, u32[]{:S(2)}, u32[]{:S(2)}) collective-permute-start(s32[128,32]{0,1:T(8,128)S(1)} %dynamic-slice_bitcast_fusion.1), channel_id=1, source_target_pairs={{0,16},{16,0},{1,17},{17,1},{2,18},{18,2},{3,19},{19,3},{4,20},{20... | collective-permute-start | bytes 49160 | tf_op jit(solution)/shard_map/ppermute | solution.py:14
  35.7 39.4 %collective-permute-start.2 = (s32[128]{0:T(128)S(1)}, s32[128]{0:T(128)S(1)}, u32[]{:S(2)}, u32[]{:S(2)}) collective-permute-start(s32[128]{0:T(128)S(1)} %fusion.33), channel_id=1, source_target_pairs={{0,16},{16,0},{1,17},{17,1},{2,18},{18,2},{3,19},{19,3},{4,20},{20... | collective-permute-start | bytes 1544 | tf_op jit(solution)/shard_map/ppermute | solution.py:14
  77.5 24.7 %collective-permute-start.1 = (bf16[16,64,512]{2,1,0:T(8,128)(2,1)S(1)}, bf16[16,64,512]{2,1,0:T(8,128)(2,1)S(1)}, u32[]{:S(2)}, u32[]{:S(2)}) collective-permute-start(bf16[16,64,512]{2,1,0:T(8,128)(2,1)S(1)} %all-to-all-done), channel_id=1, source_target_pairs={{0,1},{1,0},{2,3},{3,2},{4,5},{5,4},{6,7},{7,6},{8,9},{9,8},{10,11... | collective-permute-start | bytes 3145736 | tf_op jit(solution)/shard_map/ppermute | solution.py:14
  303.9 9.5 %copy-start.7 = (f32[256,2048]{1,0:T(8,128)S(1)}, f32[256,2048]{1,0:T(8,128)}, u32[]{:S(2)}) copy-start(f32[256,2048]{1,0:T(8,128)} %fusion.19) | copy-start | bytes 6291460
  303.9 9.5 %copy-start.17 = (f32[256,512]{1,0:T(8,128)S(1)}, f32[256,512]{1,0:T(8,128)}, u32[]{:S(2)}) copy-start(f32[256,512]{1,0:T(8,128)} %fusion.42) | copy-start | bytes 1572868
  315.9 4.0 collective-permute-start.4
  321.3 82.0 %all-gather.17.cloned.1.call-start = ((), (), s32[]{:S(2)}) async-start(), calls=%async_computation.6 | async-start | bytes 2228224 | tf_op jit(solution)/shard_map/all_gather | solution.py:151
  323.4 131.3 %all-gather.13.cloned.1.call-start = ((), (), s32[]{:S(2)}) async-start(), calls=%async_computation.4 | async-start | bytes 4456448 | tf_op jit(solution)/shard_map/all_gather | solution.py:151
  454.7 7.2 %copy-start.5 = (bf16[512,512]{1,0:T(8,128)(2,1)S(1)}, bf16[512,512]{1,0:T(8,128)(2,1)}, u32[]{:S(2)}) copy-start(bf16[512,512]{1,0:T(8,128)(2,1)} %get-tuple-element.16) | copy-start | bytes 1572868
  459.7 14.8 %collective-permute-start.5 = (bf16[256,1024]{1,0:T(8,128)(2,1)S(1)}, bf16[256,1024]{1,0:T(8,128)(2,1)S(1)}, u32[]{:S(2)}, u32[]{:S(2)}) collective-permute-start(bf16[256,1024]{1,0:T(8,128)(2,1)S(1)} %constant_dynamic-slice_fusion.2), channel_id=1, source_target_pairs={{0,1},{1,0},{2,3},{3,2},{4,5},{5,4},{6,7},{7,6},{8,9},{9,8},{10,11... | collective-permute-start | bytes 1572872 | tf_op jit(solution)/shard_map/ppermute | solution.py:14
  461.3 18.9 %collective-permute-start.6 = (bf16[256,512]{1,0:T(8,128)(2,1)S(1)}, bf16[256,512]{1,0:T(8,128)(2,1)S(1)}, u32[]{:S(2)}, u32[]{:S(2)}) collective-permute-start(bf16[256,512]{1,0:T(8,128)(2,1)S(1)} %constant_dynamic-slice_fusion.1), channel_id=1, source_target_pairs={{0,1},{1,0},{2,3},{3,2},{4,5},{5,4},{6,7},{7,6},{8,9},{9,8},{10,11... | collective-permute-start | bytes 786440 | tf_op jit(solution)/shard_map/ppermute | solution.py:14
  461.9 23.2 %collective-permute-start.7 = (bf16[256,512]{1,0:T(8,128)(2,1)S(1)}, bf16[256,512]{1,0:T(8,128)(2,1)S(1)}, u32[]{:S(2)}, u32[]{:S(2)}) collective-permute-start(bf16[256,512]{1,0:T(8,128)(2,1)S(1)} %constant_dynamic-slice_fusion), channel_id=1, source_target_pairs={{0,1},{1,0},{2,3},{3,2},{4,5},{5,4},{6,7},{7,6},{8,9},{9,8},{10,11... | collective-permute-start | bytes 786440 | tf_op jit(solution)/shard_map/ppermute | solution.py:14
  (10 other events, 30.2 us)
Sparse Core Ops, SparseCore 0:
  10.2 90.1 all-gather.8
  102.7 73.8 all-gather.10
  178.7 125.1 all-gather.6
  321.4 39.5 all-gather.14
  363.1 40.1 all-gather.16
  405.4 49.3 all-gather.12

commit v2 on v1

--- a/solution.py
+++ b/solution.py
@@ -6,7 +6,7 @@
 ACTIONS = 18
 COSINES = 64
 FRACS = 64
-PARTS = (2, 1, 1)
+PARTS = (1,)
 
 
 def rotate(value, axis, step):

time: 494 us -> 348 us (0.70)
  waiting for transfers between devices: 356 us -> 222 us
  matrix products: 46.4 us -> 31.3 us
  blocking collectives: 38.7 us -> 49.2 us
    all_gather x3 -> x1, waiting for transfers between devices: 186 us -> 93.2 us  [shards(): lax.all_gather(torso_weight[:, a:b], ('grp', 'fsdp'), axis=0, tiled=True)]
    all_gather x3 -> x1, waiting for transfers between devices: 121 us -> 79.8 us  [shards(): lax.all_gather(grad_preact, ('grp', 'fsdp'), axis=0, tiled=True)]
    psum x1, blocking collectives: 38.7 us -> 49.2 us  [shards(): counts = lax.psum(jnp.sum(onehot, axis=0), 'fsdp')]
    dot_general x3 -> x1, matrix products: 25.1 us -> 16.4 us  [shards(): preact = jnp.dot(normed, weight_columns, preferred_element_type=jnp.float32)]
    dot_general x3 -> x1, matrix products: 12.2 us -> 9.83 us  [shards(): lax.dot_general(columns_all, rows, (((0,), (0,)), ((), ())), preferred_el...]
    ppermute x8 -> x6, waiting for transfers between devices: 46.1 us -> 48.4 us  [rotate(): lax.ppermute(value, axis, [(s, (s + step) % size) for s in range(size)])]
  transfers between devices with their start and end apart: 15 -> 9, of which waited for: 12 -> 6; matrix products, arithmetic and copies ran while one was open for 9% -> 4% of each run, Pallas kernels for 0% -> 0%
where the time goes in v2:
time: 348 us
  waiting for transfers between devices  222 us (64%)
  blocking collectives  49.2 us (14%)
  matrix products  31.3 us (9%)
  between operations  14.3 us (4%)
  starting transfers between devices  13.1 us (4%)
  other arithmetic  9.72 us (3%)
  local copies, waits for them, and re-layouts  8.1 us (2%)
    all_gather x1, waiting for transfers between devices, shards(): lax.all_gather(torso_weight[:, a:b], ('grp', 'fsdp'), axis=0, tiled=True)  93.2 us
    all_gather x1, waiting for transfers between devices, shards(): lax.all_gather(grad_preact, ('grp', 'fsdp'), axis=0, tiled=True)  79.8 us
    psum x1, blocking collectives, shards(): counts = lax.psum(jnp.sum(onehot, axis=0), 'fsdp')  49.2 us
    ppermute x6, waiting for transfers between devices, rotate(): lax.ppermute(value, axis, [(s, (s + step) % size) for s in range(size)])  48.4 us
    dot_general x1, matrix products, shards(): preact = jnp.dot(normed, weight_columns, preferred_element_type=jnp.float32)  16.4 us
    dot_general x1, matrix products, shards(): lax.dot_general(columns_all, rows, (((0,), (0,)), ((), ())), preferred_el...  9.83 us
    all_to_all x1, starting transfers between devices, shards(): lax.all_to_all(outgoing, ('grp', 'fsdp'), split_axis=0, concat_axis=0, ti...  7.31 us
  transfers between devices with their start and end apart: 9, of which 6 were waited for; matrix products, arithmetic and copies ran while one was open for 4% of the time, Pallas kernels for 0%

profile of v2, /device:TPU:0, one launch (start us, length us, event | category | flops | bytes accessed | tf_op | source)
XLA Modules:
  0.0 347.8 jit_solution(14131071767026952753)
XLA Ops:
  7.9 3.1 dynamic-slice_bitcast_fusion
  11.5 4.0 %collective-permute-done = bf16[128,8192]{1,0:T(8,128)(2,1)S(1)} collective-permute-done((bf16[128,8192]{1,0:T(8,128)(2,1)}, bf16[128,8192]{1,0:T(8,128)(2,1)S(1)}, u32[]{:S(2)}, u32[]{:S(2)}) %collective-permute-start) | collective-permute-done | bytes 2097184 | tf_op jit(solution)/shard_map/ppermute | solution.py:14
  15.5 2.5 bitcast_select_fusion.1
  18.0 1.0 fusion
  19.0 1.3 fusion.2
  20.8 1.6 copy-done.3
  22.4 1.5 copy.23
  23.9 7.3 %all-to-all-start = ((bf16[16,64,512]{2,1,0:T(8,128)(2,1)}), bf16[16,64,512]{2,1,0:T(8,128)(2,1)S(1)}, u32[]{:S(2)}, u32[]{:S(2)}) async-start(bf16[16,64,512]{2,1,0:T(8,128)(2,1)} %copy.23), calls=%async_computation | async-start | bytes 2097152 | tf_op jit(solution)/shard_map/all_to_all | solution.py:91
  32.1 49.2 %psum.7 = f32[8]{0:T(128)S(1)} all-reduce(f32[8]{0:T(128)S(1)} %convert_reduce_fusion), channel_id=1, replica_groups=mesh['grp'=2,'fsdp'=8,'tp'=2] {'fsdp'}, use_global_device_ids=true, to_apply=%region_2.3 | all-reduce | flops 8 | bytes 64 | tf_op jit(solution)/shard_map/psum | solution.py:74
  81.9 1.6 collective-permute-start.1
  83.4 1.8 fusion.11
  85.9 18.1 %collective-permute-done.1 = bf16[16,64,512]{2,1,0:T(8,128)(2,1)S(1)} collective-permute-done((bf16[16,64,512]{2,1,0:T(8,128)(2,1)S(1)}, bf16[16,64,512]{2,1,0:T(8,128)(2,1)S(1)}, u32[]{:S(2)}, u32[]{:S(2)}) %collective-permute-start.1) | collective-permute-done | bytes 1048608 | tf_op jit(solution)/shard_map/ppermute | solution.py:14
  104.4 93.2 %all-gather.3.cloned.1.call-done = bf16[8192,2048]{1,0:T(8,128)(2,1)} async-done(((bf16[512,2048]{1,0:T(8,128)(2,1)}), bf16[8192,2048]{1,0:T(8,128)(2,1)}) %all-gather.3.cloned.1.call-update) | async-done | bytes 33554448 | tf_op jit(solution)/shard_map/all_gather | solution.py:66
  197.5 16.4 %fusion.24 = f32[256,2048]{1,0:T(8,128)S(1)} fusion(bf16[256,8192]{1,0:T(8,128)(2,1)} %copy-done.3, bf16[8192,2048]{1,0:T(8,128)(2,1)} %all-gather.3.cloned.1.call-done), kind=kOutput, calls=%fused_computation.68 | convolution fusion | flops 8589934592 | bytes 39845888 | tf_op jit(solution)/shard_map/dot_general | solution.py:118
  215.0 1.5 collective-permute-start.4
  216.6 2.4 collective-permute-done.4
  219.4 1.7 fusion.5
  221.1 79.8 %all-gather.5.cloned.1.call-done = bf16[2048,2048]{1,0:T(8,128)(2,1)} async-done(((bf16[128,2048]{1,0:T(8,128)(2,1)}), bf16[2048,2048]{1,0:T(8,128)(2,1)}) %all-gather.5.cloned.1.call-update) | async-done | bytes 8388624 | tf_op jit(solution)/shard_map/all_gather | solution.py:151
  301.0 9.8 %subtract_convert_fusion = (bf16[512,2048]{1,0:T(8,128)(2,1)S(1)}, f32[512,2048]{1,0:T(8,128)}) fusion(bf16[512,2048]{1,0:T(8,128)(2,1)} %param.17, bf16[2048,512]{1,0:T(8,128)(2,1)S(1)} %bitcast.52, bf16[2048,2048]{1,0:T(8,128)(2,1)} %all-gather.5.cloned.1.call-done), kind=kOutput, calls=%fused_computation.6 | convolution fusion | flops 4299161600 | bytes 18874368 | tf_op jit(solution)/shard_map/dot_general | solution.py:157
  310.8 1.3 copy-done.2
  312.2 1.5 collective-permute-start.5
  313.7 23.9 %collective-permute-done.5 = bf16[256,2048]{1,0:T(8,128)(2,1)S(1)} collective-permute-done((bf16[256,2048]{1,0:T(8,128)(2,1)S(1)}, bf16[256,2048]{1,0:T(8,128)(2,1)S(1)}, u32[]{:S(2)}, u32[]{:S(2)}) %collective-permute-start.5) | collective-permute-done | bytes 1048608 | tf_op jit(solution)/shard_map/ppermute | solution.py:14
  337.6 1.8 broadcast_select_fusion.1
  339.4 1.5 pad_maximum_fusion.2
  (60 shorter events, 5.6 us)
Async XLA Ops:
  7.2 74.2 %copy-start = (bf16[64,2048]{1,0:T(8,128)(2,1)S(1)}, bf16[64,2048]{1,0:T(8,128)(2,1)}, u32[]{:S(2)}) copy-start(bf16[64,2048]{1,0:T(8,128)(2,1)} %param.18) | copy-start | bytes 786436
  7.2 190.4 %all-gather.3.cloned.1.call-start = ((), (), s32[]{:S(2)}) async-start(), calls=%async_computation.1 | async-start | bytes 35651584 | tf_op jit(solution)/shard_map/all_gather | solution.py:66
  11.0 4.5 %collective-permute-start = (bf16[128,8192]{1,0:T(8,128)(2,1)}, bf16[128,8192]{1,0:T(8,128)(2,1)S(1)}, u32[]{:S(2)}, u32[]{:S(2)}) collective-permute-start(bf16[128,8192]{1,0:T(8,128)(2,1)} %dynamic-slice_bitcast_fusion), channel_id=1, source_target_pairs={{0,16},{16,0},{1,17},{17,1},{2,18},{18,2},{3,19},{19,3},{4,20},{20... | collective-permute-start | bytes 6291464 | tf_op jit(solution)/shard_map/ppermute | solution.py:14
  18.0 1.0 copy-start.6
  20.3 2.0 copy-start.3
  22.4 8.9 %copy-start.7 = (s32[1,256,32]{1,2,0:T(8,128)S(1)}, s32[1,256,32]{1,2,0:T(8,128)}, u32[]{:S(2)}) copy-start(s32[1,256,32]{1,2,0:T(8,128)} %param.13) | copy-start | bytes 98308
  22.4 9.4 %copy-start.10 = (s32[1,256]{1,0:T(1,128)S(1)}, s32[1,256]{1,0:T(1,128)}, u32[]{:S(2)}) copy-start(s32[1,256]{1,0:T(1,128)} %param.12) | copy-start | bytes 3076
  22.4 9.4 %copy-start.8 = (s32[256,1]{0,1:T(1,128)S(1)}, s32[256,1]{0,1:T(1,128)}, u32[]{:S(2)}) copy-start(s32[256,1]{0,1:T(1,128)} %param.14) | copy-start | bytes 3076
  22.4 59.0 %copy-start.9 = (f32[64]{0:T(128)S(1)}, f32[64]{0:T(128)}, u32[]{:S(2)}) copy-start(f32[64]{0:T(128)} %param.15) | copy-start | bytes 772
  22.4 61.0 %copy-start.5 = (bf16[18,2048]{1,0:T(8,128)(2,1)S(1)}, bf16[18,2048]{1,0:T(8,128)(2,1)}, u32[]{:S(2)}) copy-start(bf16[18,2048]{1,0:T(8,128)(2,1)} %param.19) | copy-start | bytes 221188
  23.9 57.9 %all-to-all-start = ((bf16[16,64,512]{2,1,0:T(8,128)(2,1)}), bf16[16,64,512]{2,1,0:T(8,128)(2,1)S(1)}, u32[]{:S(2)}, u32[]{:S(2)}) async-start(bf16[16,64,512]{2,1,0:T(8,128)(2,1)} %copy.23), calls=%async_computation | async-start | bytes 2097152 | tf_op jit(solution)/shard_map/all_to_all | solution.py:91
  31.2 269.7 %all-gather.5.cloned.1.call-start = ((), (), s32[]{:S(2)}) async-start(), calls=%async_computation.2 | async-start | bytes 8912896 | tf_op jit(solution)/shard_map/all_gather | solution.py:151
  31.3 53.9 %collective-permute-start.3 = (s32[128,32]{0,1:T(8,128)S(1)}, s32[128,32]{0,1:T(8,128)S(1)}, u32[]{:S(2)}, u32[]{:S(2)}) collective-permute-start(s32[128,32]{0,1:T(8,128)S(1)} %dynamic-slice_bitcast_fusion.1), channel_id=1, source_target_pairs={{0,16},{16,0},{1,17},{17,1},{2,18},{18,2},{3,19},{19,3},{4,20},{20... | collective-permute-start | bytes 49160 | tf_op jit(solution)/shard_map/ppermute | solution.py:14
  31.9 49.9 %collective-permute-start.2 = (s32[128]{0:T(128)S(1)}, s32[128]{0:T(128)S(1)}, u32[]{:S(2)}, u32[]{:S(2)}) collective-permute-start(s32[128]{0:T(128)S(1)} %fusion.19), channel_id=1, source_target_pairs={{0,16},{16,0},{1,17},{17,1},{2,18},{18,2},{3,19},{19,3},{4,20},{20... | collective-permute-start | bytes 1544 | tf_op jit(solution)/shard_map/ppermute | solution.py:14
  81.9 22.2 %collective-permute-start.1 = (bf16[16,64,512]{2,1,0:T(8,128)(2,1)S(1)}, bf16[16,64,512]{2,1,0:T(8,128)(2,1)S(1)}, u32[]{:S(2)}, u32[]{:S(2)}) collective-permute-start(bf16[16,64,512]{2,1,0:T(8,128)(2,1)S(1)} %all-to-all-done), channel_id=1, source_target_pairs={{0,1},{1,0},{2,3},{3,2},{4,5},{5,4},{6,7},{7,6},{8,9},{9,8},{10,11... | collective-permute-start | bytes 3145736 | tf_op jit(solution)/shard_map/ppermute | solution.py:14
  197.5 16.4 %copy-start.4 = (f32[256,2048]{1,0:T(8,128)S(1)}, f32[256,2048]{1,0:T(8,128)}, u32[]{:S(2)}) copy-start(f32[256,2048]{1,0:T(8,128)} %fusion.11) | copy-start | bytes 6291460
  213.9 2.6 copy-start.11
  215.0 4.0 %collective-permute-start.4 = (f32[256,32]{0,1:T(8,128)S(1)}, f32[256,32]{0,1:T(8,128)S(1)}, u32[]{:S(2)}, u32[]{:S(2)}) collective-permute-start(f32[256,32]{0,1:T(8,128)S(1)} %select_reduce_fusion), channel_id=1, source_target_pairs={{0,1},{1,0},{2,3},{3,2},{4,5},{5,4},{6,7},{7,6},{8,9},{9,8},{10,11... | collective-permute-start | bytes 98312 | tf_op jit(solution)/shard_map/ppermute | solution.py:14
  310.8 1.3 copy-start.2
  312.2 25.4 %collective-permute-start.5 = (bf16[256,2048]{1,0:T(8,128)(2,1)S(1)}, bf16[256,2048]{1,0:T(8,128)(2,1)S(1)}, u32[]{:S(2)}, u32[]{:S(2)}) collective-permute-start(bf16[256,2048]{1,0:T(8,128)(2,1)S(1)} %constant_dynamic-slice_fusion), channel_id=1, source_target_pairs={{0,1},{1,0},{2,3},{3,2},{4,5},{5,4},{6,7},{7,6},{8,9},{9,8},{10,11... | collective-permute-start | bytes 3145736 | tf_op jit(solution)/shard_map/ppermute | solution.py:14
  339.4 1.6 copy-start.1
Sparse Core Ops, SparseCore 0:
  9.6 187.8 all-gather.2
  221.3 79.6 all-gather.4

commit v3 on v2

--- a/solution.py
+++ b/solution.py
@@ -21,6 +21,37 @@
     got = rotate(sent, "grp", 1)
     first = group_index == 0
     return jnp.concatenate([jnp.where(first, kept, got), jnp.where(first, got, kept)], axis=0)
+
+
+def ring_order(total):
+    return list(range(0, total, 2)) + list(range(total - 1, 0, -2))
+
+
+def ring_gather(value, total):
+    cycle = ring_order(total)
+    ahead = [(cycle[i], cycle[(i + 1) % total]) for i in range(total)]
+    back = [(b, a) for a, b in ahead]
+    pieces, forward, backward = [value], value, value
+    for step in range(1, total // 2 + 1):
+        forward = lax.ppermute(forward, "fsdp", ahead)
+        pieces.append(forward)
+        if 2 * step < total:
+            backward = lax.ppermute(backward, "fsdp", back)
+            pieces.append(backward)
+    return pieces
+
+
+def ring_sources(total, index):
+    cycle = ring_order(total)
+    table = [None] * total
+    for place, owner in enumerate(cycle):
+        sources = [owner]
+        for step in range(1, total // 2 + 1):
+            sources.append(cycle[(place - step) % total])
+            if 2 * step < total:
+                sources.append(cycle[(place + step) % total])
+        table[owner] = sources
+    return jnp.asarray(table, dtype=jnp.int32)[index]
 
 
 def arrange(pieces, index):
@@ -92,7 +123,12 @@
     pieces = [incoming] + [rotate(incoming, "tp", step) for step in range(1, tp_total)]
     columns_all = jnp.concatenate(
         [piece[:, None] for piece in arrange(pieces, tp_index)], axis=1
-    ).reshape(2 * shard_total * half, block)
+    ).reshape(2, shard_total, half, block)
+    columns_all = jnp.take(columns_all, ring_sources(shard_total, lax.axis_index("fsdp")), axis=1)
+    columns_all = columns_all.reshape(2, shard_total * half, block)
+    columns_all = jnp.where(group_index == 0, columns_all, columns_all[::-1]).reshape(
+        2 * shard_total * half, block
+    )
 
     choose_mask = (action_rows[:, None] == jnp.arange(ACTIONS, dtype=jnp.int32)[None, :]).astype(
         jnp.bfloat16
@@ -148,7 +184,9 @@
         grad_preact = (
             grad_feature * picked[half:, a:b] * gate_value * (1.0 + preact * (1.0 - gate_value))
         ).astype(jnp.bfloat16)
-        rows_all.append(lax.all_gather(grad_preact, ("grp", "fsdp"), axis=0, tiled=True))
+        own = ring_gather(grad_preact, shard_total)
+        partner = [rotate(piece, "grp", 1) for piece in own]
+        rows_all.append(jnp.concatenate(own + partner, axis=0))
 
     grads = []
     refreshed = [[] for _ in range(tp_total)]

time: 348 us -> 330 us (0.948)
  waiting for transfers between devices: 222 us -> 167 us
  local copies, waits for them, and re-layouts: 8.1 us -> 27.4 us
  starting transfers between devices: 13.1 us -> 28.6 us
    all_gather x1 -> x0, waiting for transfers between devices: 79.8 us -> none  [shards(): lax.all_gather(grad_preact, ('grp', 'fsdp'), axis=0, tiled=True)]
    ppermute x0 -> x7, waiting for transfers between devices: none -> 31.5 us  [the longest x4 30.8 us: ring_gather(): forward = lax.ppermute(forward, 'fsdp', ahead)]
    unnamed x25 -> x43, local copies, waits for them, and re-layouts: 3.29 us -> 17.7 us
    ppermute x0 -> x7, starting transfers between devices: none -> 13.9 us  [the longest x4 13.9 us: ring_gather(): forward = lax.ppermute(forward, 'fsdp', ahead)]
    all_gather x1, waiting for transfers between devices: 93.2 us -> 86.4 us  [shards(): lax.all_gather(torso_weight[:, a:b], ('grp', 'fsdp'), axis=0, tiled=True)]
    gather x0 -> x2, local copies, waits for them, and re-layouts: none -> 3.75 us  [shards(): jnp.take(columns_all, ring_sources(shard_total, lax.axis_index('fsdp')),...]
    ppermute x6 -> x14, starting transfers between devices: 5.71 us -> 7.38 us  [rotate(): lax.ppermute(value, axis, [(s, (s + step) % size) for s in range(size)])]
    ppermute x6 -> x14, waiting for transfers between devices: 48.4 us -> 48.1 us  [rotate(): lax.ppermute(value, axis, [(s, (s + step) % size) for s in range(size)])]
  transfers between devices with their start and end apart: 9 -> 23, of which waited for: 6 -> 10; matrix products, arithmetic and copies ran while one was open for 4% -> 10% of each run, Pallas kernels for 0% -> 0%
where the time goes in v3:
time: 330 us; the launch traced here: 329 us
  waiting for transfers between devices  167 us (51%)
  blocking collectives  49.2 us (15%)
  matrix products  31 us (9%)
  starting transfers between devices  28.6 us (9%)
  local copies, waits for them, and re-layouts  27.4 us (8%)
  between operations  14.4 us (4%)
  other arithmetic  12 us (4%)
    all_gather x1, waiting for transfers between devices, shards(): lax.all_gather(torso_weight[:, a:b], ('grp', 'fsdp'), axis=0, tiled=True)  86.4 us
    psum x1, blocking collectives, shards(): counts = lax.psum(jnp.sum(onehot, axis=0), 'fsdp')  49.2 us
    ppermute x14, waiting for transfers between devices, rotate(): lax.ppermute(value, axis, [(s, (s + step) % size) for s in range(size)])  48.1 us
    ppermute x4, waiting for transfers between devices, ring_gather(): forward = lax.ppermute(forward, 'fsdp', ahead)  30.8 us
    unnamed x43, local copies, waits for them, and re-layouts  17.7 us
    dot_general x1, matrix products, shards(): preact = jnp.dot(normed, weight_columns, preferred_element_type=jnp.float32)  16.4 us
    ppermute x4, starting transfers between devices, ring_gather(): forward = lax.ppermute(forward, 'fsdp', ahead)  13.9 us
    dot_general x1, matrix products, shards(): lax.dot_general(columns_all, rows, (((0,), (0,)), ((), ())), preferred_el...  9.5 us
  transfers between devices with their start and end apart: 23, of which 10 were waited for; matrix products, arithmetic and copies ran while one was open for 10% of the time, Pallas kernels for 0%

profile of v3, /device:TPU:0, one launch (start us, length us, event | category | flops | bytes accessed | tf_op | source)
XLA Modules:
  0.0 329.3 jit_solution(8939010091441323462)
XLA Ops:
  7.9 3.1 dynamic-slice_bitcast_fusion
  11.5 4.0 %collective-permute-done = bf16[128,8192]{1,0:T(8,128)(2,1)S(1)} collective-permute-done((bf16[128,8192]{1,0:T(8,128)(2,1)}, bf16[128,8192]{1,0:T(8,128)(2,1)S(1)}, u32[]{:S(2)}, u32[]{:S(2)}) %collective-permute-start) | collective-permute-done | bytes 2097184 | tf_op jit(solution)/shard_map/ppermute | solution.py:14
  15.5 2.5 bitcast_select_fusion.2
  20.4 2.0 copy-done.4
  24.4 7.3 %all-to-all-start = ((bf16[16,64,512]{2,1,0:T(8,128)(2,1)}), bf16[16,64,512]{2,1,0:T(8,128)(2,1)S(1)}, u32[]{:S(2)}, u32[]{:S(2)}) async-start(bf16[16,64,512]{2,1,0:T(8,128)(2,1)} %copy.27), calls=%async_computation | async-start | bytes 2097152 | tf_op jit(solution)/shard_map/all_to_all | solution.py:122
  32.5 49.2 %psum.7 = f32[8]{0:T(128)S(1)} all-reduce(f32[8]{0:T(128)S(1)} %convert_reduce_fusion), channel_id=1, replica_groups=mesh['grp'=2,'fsdp'=8,'tp'=2] {'fsdp'}, use_global_device_ids=true, to_apply=%region_2.3 | all-reduce | flops 8 | bytes 64 | tf_op jit(solution)/shard_map/psum | solution.py:105
  85.3 1.8 fusion.11
  87.8 18.2 %collective-permute-done.1 = bf16[16,64,512]{2,1,0:T(8,128)(2,1)S(1)} collective-permute-done((bf16[16,64,512]{2,1,0:T(8,128)(2,1)S(1)}, bf16[16,64,512]{2,1,0:T(8,128)(2,1)S(1)}, u32[]{:S(2)}, u32[]{:S(2)}) %collective-permute-start.1) | collective-permute-done | bytes 1048608 | tf_op jit(solution)/shard_map/ppermute | solution.py:14
  106.5 2.0 gather_fusion
  111.1 86.4 %all-gather.2.cloned.1.call-done = bf16[8192,2048]{1,0:T(8,128)(2,1)} async-done(((bf16[512,2048]{1,0:T(8,128)(2,1)}), bf16[8192,2048]{1,0:T(8,128)(2,1)}) %all-gather.2.cloned.1.call-update) | async-done | bytes 33554448 | tf_op jit(solution)/shard_map/all_gather | solution.py:97
  197.5 16.4 %fusion.25 = f32[256,2048]{1,0:T(8,128)S(1)} fusion(bf16[256,8192]{1,0:T(8,128)(2,1)} %copy-done.4, bf16[8192,2048]{1,0:T(8,128)(2,1)} %all-gather.2.cloned.1.call-done), kind=kOutput, calls=%fused_computation.94 | convolution fusion | flops 8589934592 | bytes 39845888 | tf_op jit(solution)/shard_map/dot_general | solution.py:154
  216.6 2.4 collective-permute-done.4
  221.2 7.1 %collective-permute-start.5 = (bf16[128,2048]{1,0:T(8,128)(2,1)S(1)}, bf16[128,2048]{1,0:T(8,128)(2,1)}, u32[]{:S(2)}, u32[]{:S(2)}) collective-permute-start(bf16[128,2048]{1,0:T(8,128)(2,1)S(1)} %get-tuple-element.27), channel_id=1, source_target_pairs={{0,4},{4,8},{8,12},{12,14},{14,10},{10,6},{6,2},{2,0},{1,5},{5,9},... | collective-permute-start | bytes 1572872 | tf_op jit(solution)/shard_map/ppermute | solution.py:36
  228.3 10.5 %collective-permute-done.5 = bf16[128,2048]{1,0:T(8,128)(2,1)} collective-permute-done((bf16[128,2048]{1,0:T(8,128)(2,1)S(1)}, bf16[128,2048]{1,0:T(8,128)(2,1)}, u32[]{:S(2)}, u32[]{:S(2)}) %collective-permute-start.5) | collective-permute-done | bytes 524320 | tf_op jit(solution)/shard_map/ppermute | solution.py:36
  238.8 2.6 collective-permute-start.7
  242.0 9.5 %collective-permute-done.7 = bf16[128,2048]{1,0:T(8,128)(2,1)S(1)} collective-permute-done((bf16[128,2048]{1,0:T(8,128)(2,1)}, bf16[128,2048]{1,0:T(8,128)(2,1)S(1)}, u32[]{:S(2)}, u32[]{:S(2)}) %collective-permute-start.7) | collective-permute-done | bytes 524320 | tf_op jit(solution)/shard_map/ppermute | solution.py:36
  251.6 2.1 collective-permute-start.9
  253.6 1.9 constant_dynamic-update-slice_fusion.14
  255.5 1.9 constant_dynamic-update-slice_fusion.13
  258.3 5.4 %collective-permute-done.9 = bf16[128,2048]{1,0:T(8,128)(2,1)S(1)} collective-permute-done((bf16[128,2048]{1,0:T(8,128)(2,1)S(1)}, bf16[128,2048]{1,0:T(8,128)(2,1)S(1)}, u32[]{:S(2)}, u32[]{:S(2)}) %collective-permute-start.9) | collective-permute-done | bytes 524320 | tf_op jit(solution)/shard_map/ppermute | solution.py:36
  263.6 2.1 collective-permute-start.11
  269.0 5.4 %collective-permute-done.11 = bf16[128,2048]{1,0:T(8,128)(2,1)S(1)} collective-permute-done((bf16[128,2048]{1,0:T(8,128)(2,1)S(1)}, bf16[128,2048]{1,0:T(8,128)(2,1)S(1)}, u32[]{:S(2)}, u32[]{:S(2)}) %collective-permute-start.11) | collective-permute-done | bytes 524320 | tf_op jit(solution)/shard_map/ppermute | solution.py:36
  283.2 9.5 %subtract_convert_fusion = (bf16[512,2048]{1,0:T(8,128)(2,1)S(1)}, f32[512,2048]{1,0:T(8,128)}) fusion(bf16[512,2048]{1,0:T(8,128)(2,1)S(1)} %copy-done.3, bf16[2048,512]{1,0:T(8,128)(2,1)S(1)} %bitcast.62, bf16[2048,2048]{1,0:T(8,128)(2,1)} %constant_dynamic-update-slice_fusion), kind=kOutput, calls=%fused_computation.7 | convolution fusion | flops 4299161600 | bytes 18874368 | tf_op jit(solution)/shard_map/dot_general | solution.py:195
  295.6 23.6 %collective-permute-done.20 = bf16[256,2048]{1,0:T(8,128)(2,1)S(1)} collective-permute-done((bf16[256,2048]{1,0:T(8,128)(2,1)S(1)}, bf16[256,2048]{1,0:T(8,128)(2,1)S(1)}, u32[]{:S(2)}, u32[]{:S(2)}) %collective-permute-start.20) | collective-permute-done | bytes 1048608 | tf_op jit(solution)/shard_map/ppermute | solution.py:14
  (115 shorter events, 38.2 us)
Async XLA Ops:
  7.2 76.2 %copy-start = (bf16[64,2048]{1,0:T(8,128)(2,1)S(1)}, bf16[64,2048]{1,0:T(8,128)(2,1)}, u32[]{:S(2)}) copy-start(bf16[64,2048]{1,0:T(8,128)(2,1)} %param.19) | copy-start | bytes 786436
  7.2 190.4 %all-gather.2.cloned.1.call-start = ((), (), s32[]{:S(2)}) async-start(), calls=%async_computation.1 | async-start | bytes 35651584 | tf_op jit(solution)/shard_map/all_gather | solution.py:97
  11.0 4.5 %collective-permute-start = (bf16[128,8192]{1,0:T(8,128)(2,1)}, bf16[128,8192]{1,0:T(8,128)(2,1)S(1)}, u32[]{:S(2)}, u32[]{:S(2)}) collective-permute-start(bf16[128,8192]{1,0:T(8,128)(2,1)} %dynamic-slice_bitcast_fusion), channel_id=1, source_target_pairs={{0,16},{16,0},{1,17},{17,1},{2,18},{18,2},{3,19},{19,3},{4,20},{20... | collective-permute-start | bytes 6291464 | tf_op jit(solution)/shard_map/ppermute | solution.py:14
  24.4 59.4 %all-to-all-start = ((bf16[16,64,512]{2,1,0:T(8,128)(2,1)}), bf16[16,64,512]{2,1,0:T(8,128)(2,1)S(1)}, u32[]{:S(2)}, u32[]{:S(2)}) async-start(bf16[16,64,512]{2,1,0:T(8,128)(2,1)} %copy.27), calls=%async_computation | async-start | bytes 2097152 | tf_op jit(solution)/shard_map/all_to_all | solution.py:122
  31.7 55.4 %collective-permute-start.3 = (s32[128,32]{0,1:T(8,128)S(1)}, s32[128,32]{0,1:T(8,128)S(1)}, u32[]{:S(2)}, u32[]{:S(2)}) collective-permute-start(s32[128,32]{0,1:T(8,128)S(1)} %dynamic-slice_bitcast_fusion.1), channel_id=1, source_target_pairs={{0,16},{16,0},{1,17},{17,1},{2,18},{18,2},{3,19},{19,3},{4,20},{20... | collective-permute-start | bytes 49160 | tf_op jit(solution)/shard_map/ppermute | solution.py:14
  32.3 51.4 %collective-permute-start.2 = (s32[128]{0:T(128)S(1)}, s32[128]{0:T(128)S(1)}, u32[]{:S(2)}, u32[]{:S(2)}) collective-permute-start(s32[128]{0:T(128)S(1)} %fusion.19), channel_id=1, source_target_pairs={{0,16},{16,0},{1,17},{17,1},{2,18},{18,2},{3,19},{19,3},{4,20},{20... | collective-permute-start | bytes 1544 | tf_op jit(solution)/shard_map/ppermute | solution.py:14
  83.8 22.2 %collective-permute-start.1 = (bf16[16,64,512]{2,1,0:T(8,128)(2,1)S(1)}, bf16[16,64,512]{2,1,0:T(8,128)(2,1)S(1)}, u32[]{:S(2)}, u32[]{:S(2)}) collective-permute-start(bf16[16,64,512]{2,1,0:T(8,128)(2,1)S(1)} %all-to-all-done), channel_id=1, source_target_pairs={{0,1},{1,0},{2,3},{3,2},{4,5},{5,4},{6,7},{7,6},{8,9},{9,8},{10,11... | collective-permute-start | bytes 3145736 | tf_op jit(solution)/shard_map/ppermute | solution.py:14
  215.0 4.0 %collective-permute-start.4 = (f32[256,32]{0,1:T(8,128)S(1)}, f32[256,32]{0,1:T(8,128)S(1)}, u32[]{:S(2)}, u32[]{:S(2)}) collective-permute-start(f32[256,32]{0,1:T(8,128)S(1)} %select_reduce_fusion), channel_id=1, source_target_pairs={{0,1},{1,0},{2,3},{3,2},{4,5},{5,4},{6,7},{7,6},{8,9},{9,8},{10,11... | collective-permute-start | bytes 98312 | tf_op jit(solution)/shard_map/ppermute | solution.py:14
  221.2 17.6 %collective-permute-start.5 = (bf16[128,2048]{1,0:T(8,128)(2,1)S(1)}, bf16[128,2048]{1,0:T(8,128)(2,1)}, u32[]{:S(2)}, u32[]{:S(2)}) collective-permute-start(bf16[128,2048]{1,0:T(8,128)(2,1)S(1)} %get-tuple-element.27), channel_id=1, source_target_pairs={{0,4},{4,8},{8,12},{12,14},{14,10},{10,6},{6,2},{2,0},{1,5},{5,9},... | collective-permute-start | bytes 1572872 | tf_op jit(solution)/shard_map/ppermute | solution.py:36
  228.3 13.0 %collective-permute-start.6 = (bf16[128,2048]{1,0:T(8,128)(2,1)S(1)}, bf16[128,2048]{1,0:T(8,128)(2,1)}, u32[]{:S(2)}, u32[]{:S(2)}) collective-permute-start(bf16[128,2048]{1,0:T(8,128)(2,1)S(1)} %get-tuple-element.27), channel_id=1, source_target_pairs={{4,0},{8,4},{12,8},{14,12},{10,14},{6,10},{2,6},{0,2},{5,1},{9,5},... | collective-permute-start | bytes 1572872 | tf_op jit(solution)/shard_map/ppermute | solution.py:39
  238.8 12.8 %collective-permute-start.7 = (bf16[128,2048]{1,0:T(8,128)(2,1)}, bf16[128,2048]{1,0:T(8,128)(2,1)S(1)}, u32[]{:S(2)}, u32[]{:S(2)}) collective-permute-start(bf16[128,2048]{1,0:T(8,128)(2,1)} %collective-permute-done.5), channel_id=1, source_target_pairs={{0,4},{4,8},{8,12},{12,14},{14,10},{10,6},{6,2},{2,0},{1,5},{5,9},... | collective-permute-start | bytes 1572872 | tf_op jit(solution)/shard_map/ppermute | solution.py:36
  241.3 16.1 %collective-permute-start.8 = (bf16[128,2048]{1,0:T(8,128)(2,1)}, bf16[128,2048]{1,0:T(8,128)(2,1)S(1)}, u32[]{:S(2)}, u32[]{:S(2)}) collective-permute-start(bf16[128,2048]{1,0:T(8,128)(2,1)} %collective-permute-done.6), channel_id=1, source_target_pairs={{4,0},{8,4},{12,8},{14,12},{10,14},{6,10},{2,6},{0,2},{5,1},{9,5},... | collective-permute-start | bytes 1572872 | tf_op jit(solution)/shard_map/ppermute | solution.py:39
  241.4 33.9 %collective-permute-start.12 = (bf16[128,2048]{1,0:T(8,128)(2,1)}, bf16[128,2048]{1,0:T(8,128)(2,1)S(1)}, u32[]{:S(2)}, u32[]{:S(2)}) collective-permute-start(bf16[128,2048]{1,0:T(8,128)(2,1)} %copy-done.12), channel_id=1, source_target_pairs={{0,16},{16,0},{1,17},{17,1},{2,18},{18,2},{3,19},{19,3},{4,20},{20... | collective-permute-start | bytes 1572872 | tf_op jit(solution)/shard_map/ppermute | solution.py:14
  241.4 35.2 %collective-permute-start.13 = (bf16[128,2048]{1,0:T(8,128)(2,1)}, bf16[128,2048]{1,0:T(8,128)(2,1)S(1)}, u32[]{:S(2)}, u32[]{:S(2)}) collective-permute-start(bf16[128,2048]{1,0:T(8,128)(2,1)} %collective-permute-done.5), channel_id=1, source_target_pairs={{0,16},{16,0},{1,17},{17,1},{2,18},{18,2},{3,19},{19,3},{4,20},{20... | collective-permute-start | bytes 1572872 | tf_op jit(solution)/shard_map/ppermute | solution.py:14
  241.9 35.6 %collective-permute-start.14 = (bf16[128,2048]{1,0:T(8,128)(2,1)}, bf16[128,2048]{1,0:T(8,128)(2,1)S(1)}, u32[]{:S(2)}, u32[]{:S(2)}) collective-permute-start(bf16[128,2048]{1,0:T(8,128)(2,1)} %collective-permute-done.6), channel_id=1, source_target_pairs={{0,16},{16,0},{1,17},{17,1},{2,18},{18,2},{3,19},{19,3},{4,20},{20... | collective-permute-start | bytes 1572872 | tf_op jit(solution)/shard_map/ppermute | solution.py:14
  251.6 12.1 %collective-permute-start.9 = (bf16[128,2048]{1,0:T(8,128)(2,1)S(1)}, bf16[128,2048]{1,0:T(8,128)(2,1)S(1)}, u32[]{:S(2)}, u32[]{:S(2)}) collective-permute-start(bf16[128,2048]{1,0:T(8,128)(2,1)S(1)} %collective-permute-done.7), channel_id=1, source_target_pairs={{0,4},{4,8},{8,12},{12,14},{14,10},{10,6},{6,2},{2,0},{1,5},{5,9},... | collective-permute-start | bytes 1572872 | tf_op jit(solution)/shard_map/ppermute | solution.py:36
  257.4 10.7 %collective-permute-start.10 = (bf16[128,2048]{1,0:T(8,128)(2,1)S(1)}, bf16[128,2048]{1,0:T(8,128)(2,1)S(1)}, u32[]{:S(2)}, u32[]{:S(2)}) collective-permute-start(bf16[128,2048]{1,0:T(8,128)(2,1)S(1)} %collective-permute-done.8), channel_id=1, source_target_pairs={{4,0},{8,4},{12,8},{14,12},{10,14},{6,10},{2,6},{0,2},{5,1},{9,5},... | collective-permute-start | bytes 1572872 | tf_op jit(solution)/shard_map/ppermute | solution.py:39
  263.6 10.8 %collective-permute-start.11 = (bf16[128,2048]{1,0:T(8,128)(2,1)S(1)}, bf16[128,2048]{1,0:T(8,128)(2,1)S(1)}, u32[]{:S(2)}, u32[]{:S(2)}) collective-permute-start(bf16[128,2048]{1,0:T(8,128)(2,1)S(1)} %collective-permute-done.9), channel_id=1, source_target_pairs={{0,4},{4,8},{8,12},{12,14},{14,10},{10,6},{6,2},{2,0},{1,5},{5,9},... | collective-permute-start | bytes 1572872 | tf_op jit(solution)/shard_map/ppermute | solution.py:36
  268.2 10.7 %collective-permute-start.15 = (bf16[128,2048]{1,0:T(8,128)(2,1)S(1)}, bf16[128,2048]{1,0:T(8,128)(2,1)S(1)}, u32[]{:S(2)}, u32[]{:S(2)}) collective-permute-start(bf16[128,2048]{1,0:T(8,128)(2,1)S(1)} %collective-permute-done.7), channel_id=1, source_target_pairs={{0,16},{16,0},{1,17},{17,1},{2,18},{18,2},{3,19},{19,3},{4,20},{20... | collective-permute-start | bytes 1572872 | tf_op jit(solution)/shard_map/ppermute | solution.py:14
  274.4 5.3 %collective-permute-start.16 = (bf16[128,2048]{1,0:T(8,128)(2,1)S(1)}, bf16[128,2048]{1,0:T(8,128)(2,1)S(1)}, u32[]{:S(2)}, u32[]{:S(2)}) collective-permute-start(bf16[128,2048]{1,0:T(8,128)(2,1)S(1)} %collective-permute-done.8), channel_id=1, source_target_pairs={{0,16},{16,0},{1,17},{17,1},{2,18},{18,2},{3,19},{19,3},{4,20},{20... | collective-permute-start | bytes 1572872 | tf_op jit(solution)/shard_map/ppermute | solution.py:14
  275.3 5.3 %collective-permute-start.17 = (bf16[128,2048]{1,0:T(8,128)(2,1)S(1)}, bf16[128,2048]{1,0:T(8,128)(2,1)S(1)}, u32[]{:S(2)}, u32[]{:S(2)}) collective-permute-start(bf16[128,2048]{1,0:T(8,128)(2,1)S(1)} %collective-permute-done.9), channel_id=1, source_target_pairs={{0,16},{16,0},{1,17},{17,1},{2,18},{18,2},{3,19},{19,3},{4,20},{20... | collective-permute-start | bytes 1572872 | tf_op jit(solution)/shard_map/ppermute | solution.py:14
  276.7 4.7 %collective-permute-start.18 = (bf16[128,2048]{1,0:T(8,128)(2,1)S(1)}, bf16[128,2048]{1,0:T(8,128)(2,1)S(1)}, u32[]{:S(2)}, u32[]{:S(2)}) collective-permute-start(bf16[128,2048]{1,0:T(8,128)(2,1)S(1)} %collective-permute-done.10), channel_id=1, source_target_pairs={{0,16},{16,0},{1,17},{17,1},{2,18},{18,2},{3,19},{19,3},{4,20},{20... | collective-permute-start | bytes 1572872 | tf_op jit(solution)/shard_map/ppermute | solution.py:14
  277.5 4.7 %collective-permute-start.19 = (bf16[128,2048]{1,0:T(8,128)(2,1)S(1)}, bf16[128,2048]{1,0:T(8,128)(2,1)S(1)}, u32[]{:S(2)}, u32[]{:S(2)}) collective-permute-start(bf16[128,2048]{1,0:T(8,128)(2,1)S(1)} %collective-permute-done.11), channel_id=1, source_target_pairs={{0,16},{16,0},{1,17},{17,1},{2,18},{18,2},{3,19},{19,3},{4,20},{20... | collective-permute-start | bytes 1572872 | tf_op jit(solution)/shard_map/ppermute | solution.py:14
  294.1 25.1 %collective-permute-start.20 = (bf16[256,2048]{1,0:T(8,128)(2,1)S(1)}, bf16[256,2048]{1,0:T(8,128)(2,1)S(1)}, u32[]{:S(2)}, u32[]{:S(2)}) collective-permute-start(bf16[256,2048]{1,0:T(8,128)(2,1)S(1)} %constant_dynamic-slice_fusion), channel_id=1, source_target_pairs={{0,1},{1,0},{2,3},{3,2},{4,5},{5,4},{6,7},{7,6},{8,9},{9,8},{10,11... | collective-permute-start | bytes 3145736 | tf_op jit(solution)/shard_map/ppermute | solution.py:14
  (13 other events, 231.3 us)
Sparse Core Ops, SparseCore 0:
  9.6 187.8 all-gather.1
